TPU v7x, 512 devices: a whole 4x8x8 slice. The times are simulated.
512 devices in a mesh: space: 8 (over y), chan: 16 (over x, z_lo, core), rep: 4 (over z_hi).
Axes of the slice: x: 4, y: 8, z: 8 (z_hi: 4, z_lo: 2; z = z_hi * 2 + z_lo), core: 2. Of those that a mesh axis runs over, the one named last changes fastest.
Arguments:
- volume: bfloat16 [4, 192, 8, 1024], P('rep', 'chan', 'space'), may hold values from -6 to 6
- weights: bfloat16 [27, 192, 192], replicated, may hold values from -0.078125 to 0.078125
- grad_out: bfloat16 [4, 192, 8, 1024], P('rep', 'chan', 'space'), may hold values from -6 to 6
Outputs:
- conv_out: bfloat16 [4, 192, 8, 1024], P('rep', 'chan', 'space')
- grad_in: bfloat16 [4, 192, 8, 1024], P('rep', 'chan', 'space')
- grad_weights: bfloat16 [27, 192, 192], P(None, None, 'chan')
All inputs are finite; a program needn't handle non-finite values.
Results may differ from a plain program's by a relative error of at most 0.0014.
Values may be sent and summed in bfloat16 or wider, within the bound.
A program may use at most 64 MiB of HBM per device.

v0:
```python
import math

import jax
import jax.numpy as jnp
from jax import lax
from jax.sharding import PartitionSpec as P

H = 32
W = 32


OFFSETS = (-1, 0, 1)


def extended(x, sides, width):
    for axis, dim in sides:
        peers, length = (lax.axis_size(axis), x.shape[dim])
        up = [(i, (i + 1) % peers) for i in range(peers)]
        down = [(j, i) for i, j in up]
        last = lax.slice_in_dim(x, length - width, length, axis=dim)
        first = lax.slice_in_dim(x, 0, width, axis=dim)
        before = lax.ppermute(last, axis, up)
        after = lax.ppermute(first, axis, down)
        x = jnp.concatenate([before, x, after], axis=dim)
    return x


def roll_plane(source, shift_rows, shift_cols):
    leading = source.shape[:-1]
    grid = source.reshape(leading + (H, W))
    grid = jnp.roll(grid, (shift_rows, shift_cols), axis=(-2, -1))
    return grid.reshape(leading + (H * W,))


def tap_conv(tap_rows, haloed_sample, sign):
    taps, out_block, channels = tap_rows.shape
    depth = haloed_sample.shape[1] - 2
    cells = haloed_sample.shape[2]
    summed = jnp.zeros((out_block, depth, cells), jnp.float32)
    for depth_off in OFFSETS:
        start = 1 + sign * depth_off
        planes = haloed_sample[:, start : start + depth, :].reshape(channels, depth * cells)
        first = (depth_off + 1) * 9
        group = tap_rows[first : first + 9].reshape(9 * out_block, channels)
        products = jnp.dot(group, planes, preferred_element_type=jnp.float32)
        products = products.reshape(3, 3, out_block, depth, cells)
        for row_off in OFFSETS:
            for col_off in OFFSETS:
                summed = summed + roll_plane(
                    products[row_off + 1, col_off + 1], -sign * row_off, -sign * col_off
                )
    return summed


def grad_columns(haloed_sample):
    depth = haloed_sample.shape[1] - 2
    pieces = []
    for depth_off in OFFSETS:
        for row_off in OFFSETS:
            for col_off in OFFSETS:
                start = 1 - depth_off
                pieces.append(
                    roll_plane(haloed_sample[:, start : start + depth, :], row_off, col_off)
                )
    return jnp.stack(pieces)


def on_device(volume, weights, grad_out):
    samples, chan_block, depth, cells = volume.shape
    chan_index = lax.axis_index("chan")
    out_weights = lax.dynamic_slice_in_dim(weights, chan_index * chan_block, chan_block, 2)
    out_rows = jnp.transpose(out_weights, (0, 2, 1))
    haloed = extended(volume, (("space", 2),), 1)
    gathered = lax.all_gather(haloed, "chan", axis=1, tiled=True)
    grad_haloed = extended(grad_out, (("space", 2),), 1)
    outputs = [tap_conv(out_rows, gathered[0], 1).astype(jnp.bfloat16)]
    grad_cols = grad_columns(grad_haloed[0])
    interior = gathered[0, :, 1 : 1 + depth, :]
    weight_grad = jnp.einsum(
        "tczp,izp->tic", grad_cols, interior, preferred_element_type=jnp.float32
    )
    partials = [
        jnp.einsum("tic,tczp->izp", out_weights, grad_cols, preferred_element_type=jnp.float32)
    ]
    conv_out = jnp.stack(outputs)
    grad_in = lax.psum_scatter(jnp.stack(partials), "chan", scatter_dimension=1, tiled=True).astype(
        jnp.bfloat16
    )
    factor = 1.0 / math.sqrt(
        samples * lax.axis_size("rep") * depth * lax.axis_size("space") * cells
    )
    grad_weights = (lax.psum(weight_grad, ("space", "rep")) * factor).astype(jnp.bfloat16)
    return (conv_out, grad_in, grad_weights)


def solution(mesh):
    return jax.shard_map(
        on_device,
        mesh=mesh,
        in_specs=(P("rep", "chan", "space", None), P(), P("rep", "chan", "space", None)),
        out_specs=(
            P("rep", "chan", "space", None),
            P("rep", "chan", "space", None),
            P(None, None, "chan"),
        ),
        check_vma=False,
    )
```

profile of v0, /device:TPU:8, one launch (start us, length us, event | category | flops | bytes accessed | tf_op | source)
XLA Modules:
  0.0 605.8 jit_solution(16994028917517702195)
XLA Ops:
  7.2 3.6 collective-permute-start.2
  10.9 6.2 %collective-permute-start.3 = (bf16[1,12,1,1024]{3,1,2,0:T(8,128)(2,1)}, bf16[1,12,1,1024]{3,1,2,0:T(8,128)(2,1)S(1)}, u32[]{:S(2)}, u32[]{:S(2)}) collective-permute-start(bf16[1,12,1,1024]{3,1,2,0:T(8,128)(2,1)} %param.5), channel_id=1, source_target_pairs={{64,0},{128,64},{192,128},{256,192},{320,256},{384,320},{448,384},... | collective-permute-start | bytes 73736 | tf_op jit(solution)/shard_map/ppermute | solution.py:23
  18.4 1.9 collective-permute-start
  20.4 5.1 collective-permute-start.1
  27.1 2.1 copy.228
  51.7 1.7 stack_reshape.110
  55.0 1.6 stack_reshape.115
  56.6 1.6 stack_reshape.116
  58.2 1.6 stack_reshape.118
  59.9 1.6 stack_reshape.121
  61.5 1.6 stack_reshape.123
  63.1 1.6 stack_reshape.124
  64.8 1.6 stack_reshape.126
  66.4 1.6 stack_reshape.129
  68.0 1.6 stack_reshape.131
  76.4 1.7 pad_maximum_fusion.28
  82.6 5.3 stack.7
  89.3 1.7 copy.222
  91.0 142.7 %all-reduce.5 = bf16[1,192,1,1024]{3,2,0,1:T(2,128)(2,1)} all-reduce(f32[1,192,1,1024]{3,2,0,1:T(1,128)} %copy.222), channel_id=2, replica_groups=mesh['space'=8,'chan'=16,'rep'=4] {'chan'}, use_global_device_ids=true, to_apply=%region_0.1.clone | all-reduce | flops 196608 | bytes 1179648
  235.1 2.9 copy.230
  242.5 1.6 slice.747
  246.6 1.6 slice.755
  253.5 1.6 slice.782
  268.5 1.6 slice.825
  272.6 1.6 slice.752
  277.2 1.6 slice.787
  284.9 1.9 copy.171
  295.4 2.0 fusion.14
  297.4 1.7 add.352
  323.6 2.0 fusion.46
  325.6 271.6 %all-reduce.4.cloned.1.call-done = f32[27,192,12]{1,0,2:T(8,128)} async-done(((f32[27,192,12]{1,0,2:T(8,128)}), f32[27,192,12]{1,0,2:T(8,128)}) %all-reduce.4.cloned.1.call-update) | async-done | bytes 248848 | tf_op jit(solution)/shard_map/psum | solution.py:92
  597.2 1.7 multiply_convert_fusion
  (305 shorter events, 109.8 us)
Async XLA Ops:
  7.2 18.3 %copy-start = (bf16[27,192,192]{2,1,0:T(8,128)(2,1)S(1)}, bf16[27,192,192]{2,1,0:T(8,128)(2,1)}, u32[]{:S(2)}) copy-start(bf16[27,192,192]{2,1,0:T(8,128)(2,1)} %param.4) | copy-start | bytes 5971972
  7.2 228.0 %all-gather.2.cloned.1.call-start = ((), (), s32[]{:S(2)}) async-start(), calls=%async_computation | async-start | bytes 1671168 | tf_op jit(solution)/shard_map/all_gather | solution.py:74
  7.2 25.9 %collective-permute-start.2 = (bf16[1,12,1,1024]{3,1,2,0:T(8,128)(2,1)}, bf16[1,12,1,1024]{3,1,2,0:T(8,128)(2,1)S(1)}, u32[]{:S(2)}, u32[]{:S(2)}) collective-permute-start(bf16[1,12,1,1024]{3,1,2,0:T(8,128)(2,1)} %param.5), channel_id=1, source_target_pairs={{0,64},{64,128},{128,192},{192,256},{256,320},{320,384},{384,448},... | collective-permute-start | bytes 73736 | tf_op jit(solution)/shard_map/ppermute | solution.py:22
  10.9 22.3 %collective-permute-start.3 = (bf16[1,12,1,1024]{3,1,2,0:T(8,128)(2,1)}, bf16[1,12,1,1024]{3,1,2,0:T(8,128)(2,1)S(1)}, u32[]{:S(2)}, u32[]{:S(2)}) collective-permute-start(bf16[1,12,1,1024]{3,1,2,0:T(8,128)(2,1)} %param.5), channel_id=1, source_target_pairs={{64,0},{128,64},{192,128},{256,192},{320,256},{384,320},{448,384},... | collective-permute-start | bytes 73736 | tf_op jit(solution)/shard_map/ppermute | solution.py:23
  18.4 58.0 %collective-permute-start = (bf16[1,12,1,1024]{3,2,0,1:T(2,128)(2,1)}, bf16[1,12,1,1024]{3,2,0,1:T(2,128)(2,1)}, u32[]{:S(2)}, u32[]{:S(2)}) collective-permute-start(bf16[1,12,1,1024]{3,2,0,1:T(2,128)(2,1)} %copy.168), channel_id=1, source_target_pairs={{0,64},{64,128},{128,192},{192,256},{256,320},{320,384},{384,448},... | collective-permute-start | bytes 73736 | tf_op jit(solution)/shard_map/ppermute | solution.py:22
  20.4 56.1 %collective-permute-start.1 = (bf16[1,12,1,1024]{3,2,0,1:T(2,128)(2,1)}, bf16[1,12,1,1024]{3,2,0,1:T(2,128)(2,1)}, u32[]{:S(2)}, u32[]{:S(2)}) collective-permute-start(bf16[1,12,1,1024]{3,2,0,1:T(2,128)(2,1)} %copy.168), channel_id=1, source_target_pairs={{64,0},{128,64},{192,128},{256,192},{320,256},{384,320},{448,384},... | collective-permute-start | bytes 73736 | tf_op jit(solution)/shard_map/ppermute | solution.py:23
  27.1 6.0 copy-start.55
  29.2 5.7 copy-start.9
  40.1 4.0 copy-start.14
  40.8 4.0 copy-start.24
  40.8 4.0 copy-start.27
  41.6 4.0 copy-start.23
  41.6 4.0 copy-start.26
  41.7 4.6 copy-start.20
  41.7 4.6 copy-start.25
  41.7 5.4 copy-start.16
  41.7 5.4 copy-start.21
  46.3 4.6 copy-start.33
  50.1 19.5 %copy-start.29 = (bf16[12,1,32,32]{3,2,0,1:T(8,128)(2,1)S(1)}, bf16[12,1,32,32]{3,2,0,1:T(8,128)(2,1)}, u32[]{:S(2)}) copy-start(bf16[12,1,32,32]{3,2,0,1:T(8,128)(2,1)} %get-tuple-element.87) | copy-start | bytes 73732
  50.2 20.2 %copy-start.28 = (bf16[12,1,32,32]{3,2,0,1:T(8,128)(2,1)S(1)}, bf16[12,1,32,32]{3,2,0,1:T(8,128)(2,1)}, u32[]{:S(2)}) copy-start(bf16[12,1,32,32]{3,2,0,1:T(8,128)(2,1)} %get-tuple-element.88) | copy-start | bytes 73732
  50.2 21.0 %copy-start.31 = (bf16[12,1,32,32]{3,2,0,1:T(8,128)(2,1)S(1)}, bf16[12,1,32,32]{3,2,0,1:T(8,128)(2,1)}, u32[]{:S(2)}) copy-start(bf16[12,1,32,32]{3,2,0,1:T(8,128)(2,1)} %get-tuple-element.95) | copy-start | bytes 73732
  50.9 20.9 %copy-start.30 = (bf16[12,1,32,32]{3,2,0,1:T(8,128)(2,1)S(1)}, bf16[12,1,32,32]{3,2,0,1:T(8,128)(2,1)}, u32[]{:S(2)}) copy-start(bf16[12,1,32,32]{3,2,0,1:T(8,128)(2,1)} %get-tuple-element.96) | copy-start | bytes 73732
  51.7 22.6 %copy-start.32 = (bf16[12,1,32,32]{3,2,0,1:T(8,128)(2,1)S(1)}, bf16[12,1,32,32]{3,2,0,1:T(8,128)(2,1)}, u32[]{:S(2)}) copy-start(bf16[12,1,32,32]{3,2,0,1:T(8,128)(2,1)} %get-tuple-element.104) | copy-start | bytes 73732
  78.1 519.1 %all-reduce.4.cloned.1.call-start = ((), (), s32[]{:S(2)}) async-start(), calls=%async_computation.1 | async-start | bytes 786432 | tf_op jit(solution)/shard_map/psum | solution.py:92
  78.4 3.4 copy-start.50
  78.5 3.3 copy-start.49
  78.5 3.4 copy-start.48
  240.1 8.9 %copy-start.35 = (bf16[9,12,192]{2,1,0:T(8,128)(2,1)S(1)}, bf16[9,12,192]{2,1,0:T(8,128)(2,1)}, u32[]{:S(2)}) copy-start(bf16[9,12,192]{2,1,0:T(8,128)(2,1)} %copy.177) | copy-start | bytes 124420
  251.1 8.9 %copy-start.34 = (bf16[9,12,192]{2,1,0:T(8,128)(2,1)S(1)}, bf16[9,12,192]{2,1,0:T(8,128)(2,1)}, u32[]{:S(2)}) copy-start(bf16[9,12,192]{2,1,0:T(8,128)(2,1)} %copy.186) | copy-start | bytes 124420
  295.4 6.6 %copy-start.8 = (f32[12,1,31,32]{3,2,1,0:T(8,128)S(1)}, f32[12,1,31,32]{3,2,1,0:T(8,128)}, u32[]{:S(2)}) copy-start(f32[12,1,31,32]{3,2,1,0:T(8,128)} %slice.755) | copy-start | bytes 142852
  299.1 4.0 copy-start.46
  313.5 3.5 copy-start.41
  (33 other events, 70.6 us)
Sparse Core Ops, SparseCore 0:
  78.3 42.7 all-gather.1
  288.0 309.1 all-reduce.3
where the time goes:
time: 609 us; the launch traced here: 606 us
  waiting for transfers between devices  272 us (45%)
  blocking collectives  143 us (23%)
  local copies, waits for them, and re-layouts  123 us (20%)
  other arithmetic  29.8 us (5%)
  starting transfers between devices  16.9 us (3%)
  between operations  15.7 us (3%)
  matrix products  6.12 us (1%)
    psum x1, waiting for transfers between devices, on_device(): lax.psum(weight_grad, ('space', 'rep')) * factor  272 us
    unnamed x1, blocking collectives  143 us
    another operation x29, local copies, waits for them, and re-layouts, grad_columns(): return jnp.stack(pieces)  35.2 us
    slice x45, local copies, waits for them, and re-layouts, roll_plane(): grid = jnp.roll(grid, (shift_rows, shift_cols), axis=(-2, -1))  27 us
    concatenate x56, other arithmetic, roll_plane(): grid = jnp.roll(grid, (shift_rows, shift_cols), axis=(-2, -1))  22.4 us
    another operation x24, local copies, waits for them, and re-layouts, roll_plane(): grid = source.reshape(leading + (H, W))  22 us
    reshape x20, local copies, waits for them, and re-layouts, roll_plane(): return grid.reshape(leading + (H * W,))  14.5 us
  transfers between devices with their start and end apart: 6, of which 1 were waited for; matrix products, arithmetic and copies ran while one was open for 17% of the time, Pallas kernels for 0%

commit v1 on v0

v1 whole, which is shorter than its diff:
```python
import math

import jax
import jax.numpy as jnp
from jax import lax
from jax.experimental import pallas as pl
from jax.experimental.pallas import tpu as pltpu
from jax.sharding import PartitionSpec as P

H = 32
W = 32
CELLS = H * W
C = 192
BLOCK = 12
SLOT = 16
CHAN = 16
SPACE = 8
REP = 4
TAPS = 27
MEMBERS = SPACE * REP
HALF = 168
FACTOR = 1.0 / math.sqrt(4 * 8 * 1024)
MESH = pl.DeviceIdType.MESH
F32 = jnp.float32
BF16 = jnp.bfloat16


def onehot(cond):
    return jnp.where(cond, 1.0, 0.0).astype(BF16)


def iota(shape, dim):
    return lax.broadcasted_iota(jnp.int32, shape, dim)


def shift_cols(x, by):
    if by == 0:
        return x
    col = iota(x.shape, 1) & (W - 1)
    if by > 0:
        return jnp.where(col == W - 1, pltpu.roll(x, W - 1, 1), pltpu.roll(x, CELLS - 1, 1))
    return jnp.where(col == 0, pltpu.roll(x, CELLS - (W - 1), 1), pltpu.roll(x, 1, 1))


def shift_rows(x, by):
    if by == 0:
        return x
    return pltpu.roll(x, (-by * W) % CELLS, 1)


def depth_sums(rows, fields, sign, depth_off):
    first = (depth_off + 1) * 9 * SLOT
    products = jnp.dot(rows[first : first + 9 * SLOT, :], fields, preferred_element_type=F32)
    total = None
    for row_off in (-1, 0, 1):
        line = None
        for col_off in (-1, 0, 1):
            at = ((row_off + 1) * 3 + col_off + 1) * SLOT
            term = shift_cols(products[at : at + SLOT], sign * col_off)
            line = term if line is None else line + term
        line = shift_rows(line, sign * row_off)
        total = line if total is None else total + line
    return total


def position(co, tap):
    upper = co >= 6
    return jnp.where(upper, HALF + (co - 6) * TAPS, co * TAPS) + tap


def kernel(
    vol_ref, w_ref, grad_ref,
    conv_ref, gin_ref, gw_ref,
    vols, grads, halo, w_vmem, w_out, w_in, cols, out_sums, in_sums, parts, got, final,
    w_sem, vs, vr, gs, gr, fvs, fvr, fgs, fgr, hs, hr, xs, xr, rs, rr, as_, ar,
):
    space = lax.axis_index("space")
    chan = lax.axis_index("chan")
    rep = lax.axis_index("rep")
    core = lax.rem(chan, 2)
    chip = chan // 2
    sibling = chan + 1 - 2 * core
    up = lax.rem(space + 1, SPACE)
    down = lax.rem(space + SPACE - 1, SPACE)

    def chip_at(dx, dz):
        return lax.rem(chip // 2 + dx, 4) * 2 + lax.rem(chip + dz, 2)

    offsets = [(dx, dz) for dx in range(4) for dz in range(2) if dx or dz]

    def member_at(rel):
        return lax.rem(space + rel // REP, SPACE), lax.rem(rep + rel % REP, REP)

    w_copy = pltpu.make_async_copy(w_ref, w_vmem, w_sem)
    w_copy.start()

    pad = jnp.zeros((SLOT - BLOCK, CELLS), F32)
    vols[chan] = jnp.concatenate([vol_ref[...].astype(F32), pad], axis=0).astype(BF16)
    own_grad = jnp.concatenate([grad_ref[...].astype(F32), pad], axis=0)
    grads[chan] = own_grad.astype(BF16)

    barrier = pltpu.get_barrier_semaphore()
    for dx, dz in offsets:
        pl.semaphore_signal(
            barrier, inc=1, device_id={"chan": chip_at(dx, dz) * 2 + core}, device_id_type=MESH
        )
    pl.semaphore_signal(barrier, inc=1, device_id={"chan": sibling}, device_id_type=MESH)
    for rel in range(1, MEMBERS):
        y, z = member_at(rel)
        pl.semaphore_signal(barrier, inc=1, device_id={"space": y, "rep": z}, device_id_type=MESH)
    pl.semaphore_wait(barrier, 7 + 1 + MEMBERS - 1)

    def send(src, dst, s_sem, r_sem, where):
        return pltpu.make_async_remote_copy(
            src_ref=src, dst_ref=dst, send_sem=s_sem, recv_sem=r_sem,
            device_id=where, device_id_type=MESH,
        )

    halo_up = send(grads.at[chan], halo.at[0], hs.at[0], hr.at[0], {"space": up})
    halo_down = send(grads.at[chan], halo.at[1], hs.at[1], hr.at[1], {"space": down})
    halo_up.start()
    halo_down.start()

    def gather_starts(buf, s_sem, r_sem, fs_sem, fr_sem):
        copies = []
        for j, (dx, dz) in enumerate(offsets):
            c = send(buf.at[chan], buf.at[chan], s_sem.at[j], r_sem.at[j],
                     {"chan": chip_at(dx, dz) * 2 + core})
            c.start()
            copies.append(c)
        own = send(buf.at[chan], buf.at[chan], fs_sem.at[7], fr_sem.at[7], {"chan": sibling})
        own.start()
        return copies, own

    def gather_finish(buf, copies, own, fs_sem, fr_sem, r_sem, s_sem):
        forwards = []
        for j, (dx, dz) in enumerate(offsets):
            source = chip_at(4 - dx, 2 - dz) * 2 + core
            send(buf.at[source], buf.at[source], s_sem.at[j], r_sem.at[j],
                 {"chan": source}).wait_recv()
            f = send(buf.at[source], buf.at[source], fs_sem.at[j], fr_sem.at[j], {"chan": sibling})
            f.start()
            forwards.append(f)
        for j, (dx, dz) in enumerate(offsets):
            source = chip_at(4 - dx, 2 - dz) * 2 + 1 - core
            send(buf.at[source], buf.at[source], fs_sem.at[j], fr_sem.at[j],
                 {"chan": sibling}).wait_recv()
        send(buf.at[sibling], buf.at[sibling], fs_sem.at[7], fr_sem.at[7],
             {"chan": sibling}).wait_recv()
        return forwards

    v_copies, v_own = gather_starts(vols, vs, vr, fvs, fvr)
    g_copies, g_own = gather_starts(grads, gs, gr, fgs, fgr)

    lane = iota((C, CHAN * SLOT), 1)
    slot_of = onehot(
        ((lane >> 4) * BLOCK + (lane & 15) == iota((C, CHAN * SLOT), 0)) & ((lane & 15) < BLOCK)
    )
    row = iota((SLOT, C), 0)
    mine = onehot((iota((SLOT, C), 1) == chan * BLOCK + row) & (row < BLOCK))
    col = iota((2 * HALF, TAPS * SLOT), 1)
    order = onehot(
        (position(col & 15, col >> 4) == iota((2 * HALF, TAPS * SLOT), 0)) & ((col & 15) < BLOCK)
    )

    halo_up.wait_recv()
    halo_down.wait_recv()
    for depth_off in (-1, 0, 1):
        plane = own_grad if depth_off == 0 else halo[(1 - depth_off) // 2].astype(F32)
        for col_off in (-1, 0, 1):
            moved = shift_cols(plane, -col_off)
            for row_off in (-1, 0, 1):
                tap = (depth_off + 1) * 9 + (row_off + 1) * 3 + col_off + 1
                cols[tap * SLOT : (tap + 1) * SLOT, :] = shift_rows(moved, -row_off).astype(BF16)
    ordered = jnp.dot(order, cols[...], preferred_element_type=F32).astype(BF16)

    w_copy.wait()
    for tap in range(TAPS):
        at = slice(tap * SLOT, (tap + 1) * SLOT)
        w_in[at, :] = jnp.dot(
            jnp.dot(mine, w_vmem[tap], preferred_element_type=F32).astype(BF16), slot_of,
            preferred_element_type=F32,
        ).astype(BF16)
        w_out[at, :] = jnp.dot(
            lax.dot_general(
                mine, w_vmem[tap], (((1,), (1,)), ((), ())), preferred_element_type=F32
            ).astype(BF16), slot_of, preferred_element_type=F32,
        ).astype(BF16)

    v_forwards = gather_finish(vols, v_copies, v_own, fvs, fvr, vr, vs)
    fields = vols[...].reshape(CHAN * SLOT, CELLS)
    packed = jnp.dot(slot_of, fields, preferred_element_type=F32).astype(BF16)
    sums = lax.dot_general(
        ordered, packed, (((1,), (1,)), ((), ())), preferred_element_type=F32
    )
    parts[0:21] = sums[:, :128].reshape(21, 16, 128)
    side = jnp.concatenate([sums[:HALF, 128:], sums[HALF:, 128:]], axis=1)
    side = jnp.concatenate([side, jnp.zeros((8, 128), F32)], axis=0)
    parts[21:32] = side.reshape(11, 16, 128)

    scatters = []
    for rel in range(1, MEMBERS):
        y, z = member_at(rel)
        c = send(parts.at[y * REP + z], got.at[rel - 1], rs.at[rel - 1], rr.at[rel - 1],
                 {"space": y, "rep": z})
        c.start()
        scatters.append(c)

    exchanges = []

    def exchange(slot, buf, side_at, where):
        c = send(buf.at[side_at], buf.at[side_at + 2], xs.at[slot], xr.at[slot], {"space": where})
        c.start()
        exchanges.append(c)

    out_sums[0] = depth_sums(w_out, fields, 1, 1)
    exchange(0, out_sums, 0, down)
    out_sums[1] = depth_sums(w_out, fields, 1, -1)
    exchange(1, out_sums, 1, up)
    out_sums[4] = depth_sums(w_out, fields, 1, 0)

    g_forwards = gather_finish(grads, g_copies, g_own, fgs, fgr, gr, gs)
    grad_fields = grads[...].reshape(CHAN * SLOT, CELLS)
    in_sums[0] = depth_sums(w_in, grad_fields, -1, 1)
    exchange(2, in_sums, 0, up)
    in_sums[1] = depth_sums(w_in, grad_fields, -1, -1)
    exchange(3, in_sums, 1, down)

    me = space * REP + rep
    total = parts[me]
    for rel in range(1, MEMBERS):
        scatters[rel - 1].wait_recv()
        total = total + got[rel - 1]
    final[me] = (total * FACTOR).astype(BF16)
    gathers = []
    for rel in range(1, MEMBERS):
        y, z = member_at(rel)
        c = send(final.at[me], final.at[me], as_.at[rel - 1], ar.at[rel - 1],
                 {"space": y, "rep": z})
        c.start()
        gathers.append(c)

    in_sums[4] = depth_sums(w_in, grad_fields, -1, 0)
    q = iota((BLOCK * 32, 512), 0)
    at = position(q >> 5, q & 31)
    here = iota((BLOCK * 32, 512), 1)
    real = (q & 31) < TAPS
    low = onehot((at == here) & real)
    high = onehot((jnp.where(at >= HALF, at - HALF, at) + 2 * HALF == here) & real)

    for c in exchanges:
        c.wait_recv()
    conv_ref[...] = (out_sums[4] + out_sums[2] + out_sums[3])[:BLOCK].astype(BF16)
    gin_ref[...] = (in_sums[4] + in_sums[2] + in_sums[3])[:BLOCK].astype(BF16)

    for rel in range(1, MEMBERS):
        src = lax.rem(space + SPACE - rel // REP, SPACE) * REP + lax.rem(rep + REP - rel % REP, REP)
        send(final.at[src], final.at[src], as_.at[rel - 1], ar.at[rel - 1],
             {"space": up}).wait_recv()
    table = final[...].reshape(512, 128)
    left = jnp.dot(low, table, preferred_element_type=F32).astype(BF16)
    right = jnp.dot(high, table, preferred_element_type=F32)
    rows = 6 * 32
    right = jnp.concatenate([right[:rows, :64], right[rows:, 64:]], axis=0).astype(BF16)
    gw_ref[:, :, 0:128] = left.reshape(BLOCK, 32, 128)[:, :TAPS, :]
    gw_ref[:, :, 128:192] = right.reshape(BLOCK, 32, 64)[:, :TAPS, :]

    for c in (v_copies + g_copies + [v_own, g_own, halo_up, halo_down] + v_forwards
              + g_forwards + scatters + exchanges + gathers):
        c.wait_send()


def on_device(volume, weights, grad_out):
    vmem = pl.BlockSpec(memory_space=pltpu.VMEM)
    dma = pltpu.SemaphoreType.DMA
    conv, gin, gw = pl.pallas_call(
        kernel,
        out_shape=(
            jax.ShapeDtypeStruct((BLOCK, CELLS), BF16),
            jax.ShapeDtypeStruct((BLOCK, CELLS), BF16),
            jax.ShapeDtypeStruct((BLOCK, TAPS, C), BF16),
        ),
        in_specs=[vmem, pl.BlockSpec(memory_space=pl.ANY), vmem],
        out_specs=(vmem, vmem, vmem),
        scratch_shapes=[
            pltpu.VMEM((CHAN, SLOT, CELLS), BF16),
            pltpu.VMEM((CHAN, SLOT, CELLS), BF16),
            pltpu.VMEM((2, SLOT, CELLS), BF16),
            pltpu.VMEM((TAPS, C, C), BF16),
            pltpu.VMEM((TAPS * SLOT, CHAN * SLOT), BF16),
            pltpu.VMEM((TAPS * SLOT, CHAN * SLOT), BF16),
            pltpu.VMEM((TAPS * SLOT, CELLS), BF16),
            pltpu.VMEM((5, SLOT, CELLS), F32),
            pltpu.VMEM((5, SLOT, CELLS), F32),
            pltpu.VMEM((MEMBERS, 16, 128), F32),
            pltpu.VMEM((MEMBERS - 1, 16, 128), F32),
            pltpu.VMEM((MEMBERS, 16, 128), BF16),
            dma,
            dma((7,)), dma((7,)), dma((7,)), dma((7,)),
            dma((8,)), dma((8,)), dma((8,)), dma((8,)),
            dma((2,)), dma((2,)), dma((4,)), dma((4,)),
            dma((MEMBERS - 1,)), dma((MEMBERS - 1,)), dma((MEMBERS - 1,)), dma((MEMBERS - 1,)),
        ],
        compiler_params=pltpu.CompilerParams(
            collective_id=0, has_side_effects=True, vmem_limit_bytes=48 * 1024 * 1024
        ),
        cost_estimate=pl.CostEstimate(
            flops=400_000_000, bytes_accessed=3_000_000, transcendentals=0
        ),
    )(volume.reshape(BLOCK, CELLS), weights, grad_out.reshape(BLOCK, CELLS))
    shape = volume.shape
    return conv.reshape(shape), gin.reshape(shape), jnp.transpose(gw, (1, 2, 0))


def solution(mesh):
    return jax.shard_map(
        on_device,
        mesh=mesh,
        in_specs=(P("rep", "chan", "space", None), P(), P("rep", "chan", "space", None)),
        out_specs=(
            P("rep", "chan", "space", None),
            P("rep", "chan", "space", None),
            P(None, None, "chan"),
        ),
        check_vma=False,
    )
```

time: 609 us -> 54.1 us (0.09)
  the two profiles are of different devices: /device:TPU:8 before, /device:TPU:1 now
where the time goes in v1:
time: 54.1 us; the launch traced here: 53.8 us
  Pallas kernels  48 us (89%)
  local copies, waits for them, and re-layouts  5.17 us (10%)
  between operations  0.65 us (1%)
    pallas_call x1, Pallas kernels, on_device(): pl.pallas_call(kernel, out_shape=(jax.ShapeDtypeStruct((BLOCK, CELLS), BF...  48 us
    unnamed x9, local copies, waits for them, and re-layouts  5.17 us

profile of v1, /device:TPU:1, one launch (start us, length us, event | category | flops | bytes accessed | tf_op | source)
XLA Modules:
  0.0 53.8 jit_solution(3820658024044330721)
XLA Ops:
  0.6 0.0 copy-start
  0.6 1.7 %copy-done = bf16[27,192,192]{2,1,0:T(8,128)(2,1)S(1)} copy-done((bf16[27,192,192]{2,1,0:T(8,128)(2,1)S(1)}, bf16[27,192,192]{2,1,0:T(8,128)(2,1)}, u32[]{:S(2)}) %copy-start) | copy-done | bytes 1990680
  2.4 0.0 copy-start.1
  2.4 0.8 %copy-done.1 = bf16[1,12,1,1024]{3,1,2,0:T(8,128)(2,1)S(1)} copy-done((bf16[1,12,1,1024]{3,1,2,0:T(8,128)(2,1)S(1)}, bf16[1,12,1,1024]{3,1,2,0:T(8,128)(2,1)}, u32[]{:S(2)}) %copy-start.1) | copy-done | bytes 24600
  3.1 0.0 copy-start.2
  3.1 0.8 %copy-done.2 = bf16[1,12,1,1024]{3,1,2,0:T(8,128)(2,1)S(1)} copy-done((bf16[1,12,1,1024]{3,1,2,0:T(8,128)(2,1)S(1)}, bf16[1,12,1,1024]{3,1,2,0:T(8,128)(2,1)}, u32[]{:S(2)}) %copy-start.2) | copy-done | bytes 24600
  3.9 48.0 %shard_map.58 = (bf16[12,1024]{1,0:T(8,128)(2,1)S(1)}, bf16[12,1024]{1,0:T(8,128)(2,1)S(1)}, bf16[12,27,192]{2,1,0:T(8,128)(2,1)S(1)}) custom-call(bf16[12,1024]{1,0:T(8,128)(2,1)S(1)} %bitcast.6, bf16[27,192,192]{2,1,0:T(8,128)(2,1)S(1)} %copy-done, bf16[12,1024]{1,0:T(8,128)(2,1)S(1)} %bitcast.7), custom_call_target="tpu_custom_call" | custom-call | flops 400000000 | bytes 3000000 | tf_op jit(solution)/shard_map/pallas_call | solution.py:276
  51.9 0.6 %copy.9 = bf16[1,12,1,1024]{3,1,2,0:T(8,128)(2,1)} copy(bf16[1,12,1,1024]{3,1,2,0:T(8,128)(2,1)S(1)} %bitcast.9) | data formatting | bytes 49152
  52.5 0.6 %copy.10 = bf16[1,12,1,1024]{3,1,2,0:T(8,128)(2,1)} copy(bf16[1,12,1,1024]{3,1,2,0:T(8,128)(2,1)S(1)} %bitcast.8) | data formatting | bytes 49152
  53.1 0.7 %copy.11 = bf16[27,192,12]{1,0,2:T(8,128)(2,1)} copy(bf16[27,192,12]{1,0,2:T(8,128)(2,1)S(1)} %bitcast.5) | data formatting | bytes 248832
Async XLA Ops:
  0.6 1.8 %copy-start = (bf16[27,192,192]{2,1,0:T(8,128)(2,1)S(1)}, bf16[27,192,192]{2,1,0:T(8,128)(2,1)}, u32[]{:S(2)}) copy-start(bf16[27,192,192]{2,1,0:T(8,128)(2,1)} %w_ref.1) | copy-start | bytes 5971972
  2.4 0.8 %copy-start.1 = (bf16[1,12,1,1024]{3,1,2,0:T(8,128)(2,1)S(1)}, bf16[1,12,1,1024]{3,1,2,0:T(8,128)(2,1)}, u32[]{:S(2)}) copy-start(bf16[1,12,1,1024]{3,1,2,0:T(8,128)(2,1)} %param.3) | copy-start | bytes 73732
  3.1 0.8 %copy-start.2 = (bf16[1,12,1,1024]{3,1,2,0:T(8,128)(2,1)S(1)}, bf16[1,12,1,1024]{3,1,2,0:T(8,128)(2,1)}, u32[]{:S(2)}) copy-start(bf16[1,12,1,1024]{3,1,2,0:T(8,128)(2,1)} %param.5) | copy-start | bytes 73732

commit v2 on v1

v2 whole, which is shorter than its diff:
```python
import math

import jax
import jax.numpy as jnp
from jax import lax
from jax.experimental import pallas as pl
from jax.experimental.pallas import tpu as pltpu
from jax.sharding import PartitionSpec as P

H = 32
W = 32
CELLS = H * W
C = 192
BLOCK = 12
SLOT = 16
CHAN = 16
SPACE = 8
REP = 4
TAPS = 27
MEMBERS = SPACE * REP
MAIN = 243
SIDE = 81
FACTOR = 1.0 / math.sqrt(4 * 8 * 1024)
MESH = pl.DeviceIdType.MESH
F32 = jnp.float32
BF16 = jnp.bfloat16
FIRST = ((0, 1), (1, 0), (1, 1))
SECOND = ((3, 0), (3, 1), (2, 0), (2, 1))


def onehot(cond):
    return jnp.where(cond, 1.0, 0.0).astype(BF16)


def iota(shape, dim):
    return lax.broadcasted_iota(jnp.int32, shape, dim)


def dot(a, b):
    return jnp.dot(a, b, preferred_element_type=F32)


def dot_nt(a, b):
    return lax.dot_general(a, b, (((1,), (1,)), ((), ())), preferred_element_type=F32)


def shift_cols(x, by):
    if by == 0:
        return x
    col = iota(x.shape, 1) & (W - 1)
    if by > 0:
        return jnp.where(col == W - 1, pltpu.roll(x, W - 1, 1), pltpu.roll(x, CELLS - 1, 1))
    return jnp.where(col == 0, pltpu.roll(x, CELLS - (W - 1), 1), pltpu.roll(x, 1, 1))


def shift_rows(x, by):
    if by == 0:
        return x
    return pltpu.roll(x, (-by * W) % CELLS, 1)


def depth_sums(rows, fields, sign, depth_off):
    first = (depth_off + 1) * 9 * SLOT
    products = dot(rows[first : first + 9 * SLOT, :], fields)
    total = None
    for row_off in (-1, 0, 1):
        line = None
        for col_off in (-1, 0, 1):
            at = ((row_off + 1) * 3 + col_off + 1) * SLOT
            term = shift_cols(products[at : at + SLOT], sign * col_off)
            line = term if line is None else line + term
        line = shift_rows(line, sign * row_off)
        total = line if total is None else total + line
    return total


def divide(x, by, below):
    out = jnp.zeros_like(x)
    for k in range(by, below, by):
        out = out + jnp.where(x >= k, 1, 0)
    return out


def kernel(
    vol_ref, w_ref, grad_ref,
    conv_ref, gin_ref, gw_ref,
    vol_in, grad_in, vols, grads, halo, w_vmem, w_out, w_in, cols, out_sums, in_sums,
    parts, got, final,
    in_sem, vs, vr, gs, gr, fvs, fvr, fgs, fgr, hs, hr, xs, xr, rs, rr, as_, ar,
):
    space = lax.axis_index("space")
    chan = lax.axis_index("chan")
    rep = lax.axis_index("rep")
    core = lax.rem(chan, 2)
    z_lo = lax.rem(chan // 2, 2)
    x_at = chan // 4
    sibling = chan + 1 - 2 * core
    up = lax.rem(space + 1, SPACE)
    down = lax.rem(space + SPACE - 1, SPACE)
    me = space * REP + rep

    vol_copy = pltpu.make_async_copy(vol_ref, vol_in, in_sem.at[0])
    grad_copy = pltpu.make_async_copy(grad_ref, grad_in, in_sem.at[1])
    w_copy = pltpu.make_async_copy(w_ref, w_vmem, in_sem.at[2])
    vol_copy.start()
    grad_copy.start()
    w_copy.start()

    def chip_at(dx, dz):
        return lax.rem(x_at + dx, 4) * 4 + lax.rem(z_lo + dz, 2) * 2 + core

    barrier = pltpu.get_barrier_semaphore()
    for dx, dz in FIRST + SECOND:
        pl.semaphore_signal(barrier, inc=1, device_id={"chan": chip_at(dx, dz)}, device_id_type=MESH)
    pl.semaphore_signal(barrier, inc=1, device_id={"chan": sibling}, device_id_type=MESH)
    for rel in range(1, MEMBERS):
        pl.semaphore_signal(
            barrier, inc=1,
            device_id={
                "space": lax.rem(space + rel // REP, SPACE), "rep": lax.rem(rep + rel % REP, REP)
            },
            device_id_type=MESH,
        )

    pad = jnp.zeros((SLOT - BLOCK, CELLS), F32)
    vol_copy.wait()
    vols[0] = jnp.concatenate([vol_in[...].astype(F32), pad], axis=0).astype(BF16)
    grad_copy.wait()
    own_grad = jnp.concatenate([grad_in[...].astype(F32), pad], axis=0)
    grads[0] = own_grad.astype(BF16)
    pl.semaphore_wait(barrier, 7 + 1 + MEMBERS - 1)

    def send(src, dst, s_sem, r_sem, where):
        return pltpu.make_async_remote_copy(
            src_ref=src, dst_ref=dst, send_sem=s_sem, recv_sem=r_sem,
            device_id=where, device_id_type=MESH,
        )

    def to_peer(buf, dx, dz, s_sem, r_sem):
        slot = dx * 4 + dz * 2
        return send(buf.at[0], buf.at[slot], s_sem.at[slot // 2], r_sem.at[slot // 2],
                    {"chan": chip_at(4 - dx, dz)})

    def to_sibling(buf, dx, dz, s_sem, r_sem):
        slot = dx * 4 + dz * 2
        return send(buf.at[slot], buf.at[slot + 1], s_sem.at[slot // 2], r_sem.at[slot // 2],
                    {"chan": sibling})

    started = []

    def go(copy):
        copy.start()
        started.append(copy)

    def pass_on(buf, group, sems):
        s_sem, r_sem, fs_sem, fr_sem = sems
        for dx, dz in group:
            to_peer(buf, dx, dz, s_sem, r_sem).wait_recv()
            go(to_sibling(buf, dx, dz, fs_sem, fr_sem))
        for dx, dz in group:
            to_sibling(buf, dx, dz, fs_sem, fr_sem).wait_recv()

    v_sems = (vs, vr, fvs, fvr)
    g_sems = (gs, gr, fgs, fgr)
    for dx, dz in FIRST:
        go(to_peer(vols, dx, dz, vs, vr))
    go(to_sibling(vols, 0, 0, fvs, fvr))
    halo_up = send(grads.at[0], halo.at[0], hs.at[0], hr.at[0], {"space": up})
    halo_down = send(grads.at[0], halo.at[1], hs.at[1], hr.at[1], {"space": down})
    go(halo_up)
    go(halo_down)
    for dx, dz in SECOND:
        go(to_peer(vols, dx, dz, vs, vr))

    row = iota((328, TAPS * SLOT), 0)
    col = iota((328, TAPS * SLOT), 1)
    order = onehot(((col & 15) * TAPS + (col >> 4) == row) & ((col & 15) < BLOCK))
    row = iota((96, 128), 0)
    col = iota((96, 128), 1)
    compact = onehot(((col >> 4) * BLOCK + (col & 15) == row) & ((col & 15) < BLOCK))

    def columns(depth_off, plane):
        for col_off in (-1, 0, 1):
            moved = shift_cols(plane, -col_off)
            for row_off in (-1, 0, 1):
                tap = (depth_off + 1) * 9 + (row_off + 1) * 3 + col_off + 1
                cols[tap * SLOT : (tap + 1) * SLOT, :] = shift_rows(moved, -row_off).astype(BF16)

    columns(0, own_grad)
    halo_up.wait_recv()
    columns(1, halo[0].astype(F32))
    halo_down.wait_recv()
    columns(-1, halo[1].astype(F32))
    ordered = dot(order, cols[...]).astype(BF16)

    def scatter(half):
        fields = vols[8 * half : 8 * half + 8].reshape(8 * SLOT, CELLS)
        packed = dot(compact, fields).astype(BF16)
        sums = dot_nt(ordered, packed)
        side = sums[MAIN : MAIN + SIDE]
        side = jnp.concatenate(
            [side[:, 0:32], side[:, 32:64], side[:, 64:96], jnp.zeros((13, 32), F32)], axis=0
        )
        parts[16 * half : 16 * half + 16] = jnp.concatenate([sums[:256], side], axis=1).reshape(
            16, 16, 128
        )
        for k in range(4):
            pair = lax.rem(space // 2 + k, 4)
            for dz in range(REP):
                y, z = 2 * pair + half, lax.rem(rep + dz, REP)
                copy = send(parts.at[16 * half + pair * REP + z], got.at[me], rs, rr,
                            {"space": y, "rep": z})
                if k == 0 and dz == 0:
                    pl.when(y != space)(copy.start)
                else:
                    copy.start()

    to_sibling(vols, 0, 0, fvs, fvr).wait_recv()
    pass_on(vols, FIRST, v_sems)
    scatter(0)
    pass_on(vols, SECOND, v_sems)
    scatter(1)

    for dx, dz in FIRST + SECOND:
        go(to_peer(grads, dx, dz, gs, gr))
    go(to_sibling(grads, 0, 0, fgs, fgr))

    lane = iota((C, CHAN * SLOT), 1)
    at_x = (x_at + (lane >> 6)) & 3
    at_z = (z_lo + (lane >> 5)) & 1
    at_core = (core + (lane >> 4)) & 1
    block = (at_x * 4 + at_z * 2 + at_core) * BLOCK
    slot_of = onehot((block + (lane & 15) == iota((C, CHAN * SLOT), 0)) & ((lane & 15) < BLOCK))
    row = iota((SLOT, C), 0)
    mine = onehot((iota((SLOT, C), 1) == chan * BLOCK + row) & (row < BLOCK))
    w_copy.wait()
    picked = [dot_nt(mine, w_vmem[tap]).astype(BF16) for tap in range(TAPS)]
    w_out[...] = dot(jnp.concatenate(picked, axis=0), slot_of).astype(BF16)

    def exchange(slot, buf, side_at, where):
        go(send(buf.at[side_at], buf.at[side_at + 2], xs.at[slot], xr.at[slot], {"space": where}))

    fields = vols[...].reshape(CHAN * SLOT, CELLS)
    out_sums[0] = depth_sums(w_out, fields, 1, 1)
    exchange(0, out_sums, 0, down)
    out_sums[1] = depth_sums(w_out, fields, 1, -1)
    exchange(1, out_sums, 1, up)

    piece = lax.rem(space, 2) * 16 + (space // 2) * REP + rep
    got[me] = parts[piece]
    bulk = pl.ds(0, MEMBERS - 1)
    send(got.at[bulk], got.at[bulk], rs, rr, {"space": up}).wait_recv()
    final[piece] = (jnp.sum(got[...], axis=0) * FACTOR).astype(BF16)
    for rel in range(1, MEMBERS):
        send(final.at[piece], final.at[piece], as_, ar, {
            "space": lax.rem(space + rel // REP, SPACE), "rep": lax.rem(rep + rel % REP, REP)
        }).start()

    picked = [dot(mine, w_vmem[tap]).astype(BF16) for tap in range(TAPS)]
    w_in[...] = dot(jnp.concatenate(picked, axis=0), slot_of).astype(BF16)
    to_sibling(grads, 0, 0, fgs, fgr).wait_recv()
    pass_on(grads, FIRST + SECOND, g_sems)
    grad_fields = grads[...].reshape(CHAN * SLOT, CELLS)
    in_sums[0] = depth_sums(w_in, grad_fields, -1, 1)
    exchange(2, in_sums, 0, up)
    in_sums[1] = depth_sums(w_in, grad_fields, -1, -1)
    exchange(3, in_sums, 1, down)
    out_sums[4] = depth_sums(w_out, fields, 1, 0)
    in_sums[4] = depth_sums(w_in, grad_fields, -1, 0)

    row = iota((9 * 32, 256), 0)
    main_rows = onehot(
        ((row >> 5) * TAPS + (row & 31) == iota((9 * 32, 256), 1)) & ((row & 31) < TAPS)
    )
    row = iota((3 * 32, 256), 0)
    side_at = (row >> 5) * TAPS + (row & 31)
    side_rows = [
        onehot((side_at + SIDE * j == iota((3 * 32, 256), 1)) & ((row & 31) < TAPS))
        for j in range(3)
    ]

    def lanes(half, index):
        slot = divide(index, BLOCK, 96)
        to_x = (x_at + 2 * half + (slot >> 2)) & 3
        to_z = (z_lo + (slot >> 1)) & 1
        to_core = (core + slot) & 1
        return (to_x * 4 + to_z * 2 + to_core) * BLOCK + index - slot * BLOCK

    lane = iota((128, 1), 0)
    target = iota((128, C), 1)
    main_lanes = [onehot((lanes(h, lane) == target) & (lane < 96)) for h in range(2)]
    side_lanes = [
        [onehot((lanes(h, jnp.maximum(lane - 96, 0) + 32 * j) == target) & (lane >= 96))
         for j in range(3)]
        for h in range(2)
    ]

    for slot, buf in ((0, out_sums), (1, out_sums), (2, in_sums), (3, in_sums)):
        side = slot % 2
        send(buf.at[side], buf.at[side + 2], xs.at[slot], xr.at[slot], {"space": up}).wait_recv()
    conv_ref[...] = (out_sums[4] + out_sums[2] + out_sums[3])[:BLOCK].astype(BF16)
    gin_ref[...] = (in_sums[4] + in_sums[2] + in_sums[3])[:BLOCK].astype(BF16)

    send(final.at[bulk], final.at[bulk], as_, ar, {"space": up}).wait_recv()
    main = jnp.zeros((9 * 32, C), F32)
    side = jnp.zeros((3 * 32, C), F32)
    for h in range(2):
        table = final[16 * h : 16 * h + 16].reshape(256, 128)
        main = main + dot(dot(main_rows, table).astype(BF16), main_lanes[h])
        for j in range(3):
            side = side + dot(dot(side_rows[j], table).astype(BF16), side_lanes[h][j])
    gw_ref[0:9] = main.astype(BF16).reshape(9, 32, C)[:, :TAPS, :]
    gw_ref[9:12] = side.astype(BF16).reshape(3, 32, C)[:, :TAPS, :]

    for copy in started:
        copy.wait_send()
    send(got.at[bulk], got.at[bulk], rs, rr, {"space": up}).wait_send()
    send(final.at[bulk], final.at[bulk], as_, ar, {"space": up}).wait_send()


def on_device(volume, weights, grad_out):
    vmem = pl.BlockSpec(memory_space=pltpu.VMEM)
    hbm = pl.BlockSpec(memory_space=pltpu.HBM)
    dma = pltpu.SemaphoreType.DMA
    conv, gin, gw = pl.pallas_call(
        kernel,
        out_shape=(
            jax.ShapeDtypeStruct((BLOCK, CELLS), BF16),
            jax.ShapeDtypeStruct((BLOCK, CELLS), BF16),
            jax.ShapeDtypeStruct((BLOCK, TAPS, C), BF16),
        ),
        in_specs=[hbm, hbm, hbm],
        out_specs=(vmem, vmem, vmem),
        scratch_shapes=[
            pltpu.VMEM((BLOCK, CELLS), BF16),
            pltpu.VMEM((BLOCK, CELLS), BF16),
            pltpu.VMEM((CHAN, SLOT, CELLS), BF16),
            pltpu.VMEM((CHAN, SLOT, CELLS), BF16),
            pltpu.VMEM((2, SLOT, CELLS), BF16),
            pltpu.VMEM((TAPS, C, C), BF16),
            pltpu.VMEM((TAPS * SLOT, CHAN * SLOT), BF16),
            pltpu.VMEM((TAPS * SLOT, CHAN * SLOT), BF16),
            pltpu.VMEM((TAPS * SLOT, CELLS), BF16),
            pltpu.VMEM((5, SLOT, CELLS), F32),
            pltpu.VMEM((5, SLOT, CELLS), F32),
            pltpu.VMEM((MEMBERS, 16, 128), F32),
            pltpu.VMEM((MEMBERS, 16, 128), F32),
            pltpu.VMEM((MEMBERS, 16, 128), BF16),
            dma((3,)),
            dma((8,)), dma((8,)), dma((8,)), dma((8,)),
            dma((8,)), dma((8,)), dma((8,)), dma((8,)),
            dma((2,)), dma((2,)), dma((4,)), dma((4,)),
            dma, dma, dma, dma,
        ],
        compiler_params=pltpu.CompilerParams(
            collective_id=0, has_side_effects=True, vmem_limit_bytes=40 * 1024 * 1024
        ),
        cost_estimate=pl.CostEstimate(
            flops=400_000_000, bytes_accessed=3_000_000, transcendentals=0
        ),
    )(volume.reshape(BLOCK, CELLS), weights, grad_out.reshape(BLOCK, CELLS))
    shape = volume.shape
    return conv.reshape(shape), gin.reshape(shape), jnp.transpose(gw, (1, 2, 0))


def solution(mesh):
    return jax.shard_map(
        on_device,
        mesh=mesh,
        in_specs=(P("rep", "chan", "space", None), P(), P("rep", "chan", "space", None)),
        out_specs=(
            P("rep", "chan", "space", None),
            P("rep", "chan", "space", None),
            P(None, None, "chan"),
        ),
        check_vma=False,
    )
```

time: 54.1 us -> 50.4 us (0.932)
  Pallas kernels: 48 us -> 44.3 us
    pallas_call x1, Pallas kernels: 48 us -> 44.3 us  [on_device(): pl.pallas_call(kernel, out_shape=(jax.ShapeDtypeStruct((BLOCK, CELLS), BF...]
where the time goes in v2:
time: 50.4 us; the launch traced here: 50.1 us
  Pallas kernels  44.3 us (88%)
  local copies, waits for them, and re-layouts  5.17 us (10%)
  between operations  0.65 us (1%)
    pallas_call x1, Pallas kernels, on_device(): pl.pallas_call(kernel, out_shape=(jax.ShapeDtypeStruct((BLOCK, CELLS), BF...  44.3 us
    unnamed x9, local copies, waits for them, and re-layouts  5.17 us

profile of v2, /device:TPU:1, one launch (start us, length us, event | category | flops | bytes accessed | tf_op | source)
XLA Modules:
  0.0 50.1 jit_solution(15235128784725587695)
XLA Ops:
  0.6 0.0 copy-start
  0.6 1.7 %copy-done = bf16[27,192,192]{2,1,0:T(8,128)(2,1)S(1)} copy-done((bf16[27,192,192]{2,1,0:T(8,128)(2,1)S(1)}, bf16[27,192,192]{2,1,0:T(8,128)(2,1)}, u32[]{:S(2)}) %copy-start) | copy-done | bytes 1990680
  2.4 0.0 copy-start.1
  2.4 0.8 %copy-done.1 = bf16[1,12,1,1024]{3,1,2,0:T(8,128)(2,1)S(1)} copy-done((bf16[1,12,1,1024]{3,1,2,0:T(8,128)(2,1)S(1)}, bf16[1,12,1,1024]{3,1,2,0:T(8,128)(2,1)}, u32[]{:S(2)}) %copy-start.1) | copy-done | bytes 24600
  3.1 0.0 copy-start.2
  3.1 0.8 %copy-done.2 = bf16[1,12,1,1024]{3,1,2,0:T(8,128)(2,1)S(1)} copy-done((bf16[1,12,1,1024]{3,1,2,0:T(8,128)(2,1)S(1)}, bf16[1,12,1,1024]{3,1,2,0:T(8,128)(2,1)}, u32[]{:S(2)}) %copy-start.2) | copy-done | bytes 24600
  3.9 44.3 %shard_map.58 = (bf16[12,1024]{1,0:T(8,128)(2,1)S(1)}, bf16[12,1024]{1,0:T(8,128)(2,1)S(1)}, bf16[12,27,192]{2,1,0:T(8,128)(2,1)S(1)}) custom-call(bf16[12,1024]{1,0:T(8,128)(2,1)S(1)} %bitcast.6, bf16[27,192,192]{2,1,0:T(8,128)(2,1)S(1)} %copy-done, bf16[12,1024]{1,0:T(8,128)(2,1)S(1)} %bitcast.7), custom_call_target="tpu_custom_call" | custom-call | flops 400000000 | bytes 3000000 | tf_op jit(solution)/shard_map/pallas_call | solution.py:325
  48.2 0.6 %copy.9 = bf16[1,12,1,1024]{3,1,2,0:T(8,128)(2,1)} copy(bf16[1,12,1,1024]{3,1,2,0:T(8,128)(2,1)S(1)} %bitcast.9) | data formatting | bytes 49152
  48.9 0.6 %copy.10 = bf16[1,12,1,1024]{3,1,2,0:T(8,128)(2,1)} copy(bf16[1,12,1,1024]{3,1,2,0:T(8,128)(2,1)S(1)} %bitcast.8) | data formatting | bytes 49152
  49.5 0.7 %copy.11 = bf16[27,192,12]{1,0,2:T(8,128)(2,1)} copy(bf16[27,192,12]{1,0,2:T(8,128)(2,1)S(1)} %bitcast.5) | data formatting | bytes 248832
Async XLA Ops:
  0.6 1.8 %copy-start = (bf16[27,192,192]{2,1,0:T(8,128)(2,1)S(1)}, bf16[27,192,192]{2,1,0:T(8,128)(2,1)}, u32[]{:S(2)}) copy-start(bf16[27,192,192]{2,1,0:T(8,128)(2,1)} %w_ref.1) | copy-start | bytes 5971972
  2.4 0.8 %copy-start.1 = (bf16[1,12,1,1024]{3,1,2,0:T(8,128)(2,1)S(1)}, bf16[1,12,1,1024]{3,1,2,0:T(8,128)(2,1)}, u32[]{:S(2)}) copy-start(bf16[1,12,1,1024]{3,1,2,0:T(8,128)(2,1)} %param.3) | copy-start | bytes 73732
  3.1 0.8 %copy-start.2 = (bf16[1,12,1,1024]{3,1,2,0:T(8,128)(2,1)S(1)}, bf16[1,12,1,1024]{3,1,2,0:T(8,128)(2,1)}, u32[]{:S(2)}) copy-start(bf16[1,12,1,1024]{3,1,2,0:T(8,128)(2,1)} %param.5) | copy-start | bytes 73732

commit v3 on v2

--- a/solution.py
+++ b/solution.py
@@ -171,6 +171,9 @@
     go(halo_down)
     for dx, dz in SECOND:
         go(to_peer(vols, dx, dz, vs, vr))
+    for dx, dz in FIRST + SECOND:
+        go(to_peer(grads, dx, dz, gs, gr))
+    go(to_sibling(grads, 0, 0, fgs, fgr))
 
     row = iota((328, TAPS * SLOT), 0)
     col = iota((328, TAPS * SLOT), 1)
@@ -218,13 +221,6 @@
     to_sibling(vols, 0, 0, fvs, fvr).wait_recv()
     pass_on(vols, FIRST, v_sems)
     scatter(0)
-    pass_on(vols, SECOND, v_sems)
-    scatter(1)
-
-    for dx, dz in FIRST + SECOND:
-        go(to_peer(grads, dx, dz, gs, gr))
-    go(to_sibling(grads, 0, 0, fgs, fgr))
-
     lane = iota((C, CHAN * SLOT), 1)
     at_x = (x_at + (lane >> 6)) & 3
     at_z = (z_lo + (lane >> 5)) & 1
@@ -236,6 +232,26 @@
     w_copy.wait()
     picked = [dot_nt(mine, w_vmem[tap]).astype(BF16) for tap in range(TAPS)]
     w_out[...] = dot(jnp.concatenate(picked, axis=0), slot_of).astype(BF16)
+    pass_on(vols, SECOND, v_sems)
+    scatter(1)
+    picked = [dot(mine, w_vmem[tap]).astype(BF16) for tap in range(TAPS)]
+    w_in[...] = dot(jnp.concatenate(picked, axis=0), slot_of).astype(BF16)
+
+    piece = lax.rem(space, 2) * 16 + (space // 2) * REP + rep
+    bulk = pl.ds(0, MEMBERS - 1)
+
+    def reduce_piece():
+        got[me] = parts[piece]
+        send(got.at[bulk], got.at[bulk], rs, rr, {"space": up}).wait_recv()
+        final[piece] = (jnp.sum(got[...], axis=0) * FACTOR).astype(BF16)
+        for rel in range(1, MEMBERS):
+            send(final.at[piece], final.at[piece], as_, ar, {
+                "space": lax.rem(space + rel // REP, SPACE), "rep": lax.rem(rep + rel % REP, REP)
+            }).start()
+
+    even = lax.rem(space, 2) == 0
+    pl.when(even)(reduce_piece)
+
 
     def exchange(slot, buf, side_at, where):
         go(send(buf.at[side_at], buf.at[side_at + 2], xs.at[slot], xr.at[slot], {"space": where}))
@@ -246,18 +262,6 @@
     out_sums[1] = depth_sums(w_out, fields, 1, -1)
     exchange(1, out_sums, 1, up)
 
-    piece = lax.rem(space, 2) * 16 + (space // 2) * REP + rep
-    got[me] = parts[piece]
-    bulk = pl.ds(0, MEMBERS - 1)
-    send(got.at[bulk], got.at[bulk], rs, rr, {"space": up}).wait_recv()
-    final[piece] = (jnp.sum(got[...], axis=0) * FACTOR).astype(BF16)
-    for rel in range(1, MEMBERS):
-        send(final.at[piece], final.at[piece], as_, ar, {
-            "space": lax.rem(space + rel // REP, SPACE), "rep": lax.rem(rep + rel % REP, REP)
-        }).start()
-
-    picked = [dot(mine, w_vmem[tap]).astype(BF16) for tap in range(TAPS)]
-    w_in[...] = dot(jnp.concatenate(picked, axis=0), slot_of).astype(BF16)
     to_sibling(grads, 0, 0, fgs, fgr).wait_recv()
     pass_on(grads, FIRST + SECOND, g_sems)
     grad_fields = grads[...].reshape(CHAN * SLOT, CELLS)
@@ -265,6 +269,7 @@
     exchange(2, in_sums, 0, up)
     in_sums[1] = depth_sums(w_in, grad_fields, -1, -1)
     exchange(3, in_sums, 1, down)
+    pl.when(jnp.logical_not(even))(reduce_piece)
     out_sums[4] = depth_sums(w_out, fields, 1, 0)
     in_sums[4] = depth_sums(w_in, grad_fields, -1, 0)
 
@@ -316,6 +321,19 @@
         copy.wait_send()
     send(got.at[bulk], got.at[bulk], rs, rr, {"space": up}).wait_send()
     send(final.at[bulk], final.at[bulk], as_, ar, {"space": up}).wait_send()
+
+
+def store(conv_ref, gin_ref, gw_ref, conv_out, gin_out, gw_out, sems):
+    copies = [
+        pltpu.make_async_copy(src, dst, sems.at[i])
+        for i, (src, dst) in enumerate(
+            ((gw_ref, gw_out), (conv_ref, conv_out), (gin_ref, gin_out))
+        )
+    ]
+    for copy in copies:
+        copy.start()
+    for copy in copies:
+        copy.wait()
 
 
 def on_device(volume, weights, grad_out):
@@ -353,12 +371,20 @@
             dma, dma, dma, dma,
         ],
         compiler_params=pltpu.CompilerParams(
-            collective_id=0, has_side_effects=True, vmem_limit_bytes=40 * 1024 * 1024
+            collective_id=0, has_side_effects=True, vmem_limit_bytes=54000 * 1024
         ),
         cost_estimate=pl.CostEstimate(
             flops=400_000_000, bytes_accessed=3_000_000, transcendentals=0
         ),
-    )(volume.reshape(BLOCK, CELLS), weights, grad_out.reshape(BLOCK, CELLS))
+    )(*(pltpu.with_memory_space_constraint(a, pltpu.HBM) for a in
+        (volume.reshape(BLOCK, CELLS), weights, grad_out.reshape(BLOCK, CELLS))))
+    conv, gin, gw = pl.pallas_call(
+        store,
+        out_shape=tuple(jax.ShapeDtypeStruct(a.shape, a.dtype) for a in (conv, gin, gw)),
+        in_specs=[vmem, vmem, vmem],
+        out_specs=(hbm, hbm, hbm),
+        scratch_shapes=[dma((3,))],
+    )(*(pltpu.with_memory_space_constraint(a, pltpu.VMEM) for a in (conv, gin, gw)))
     shape = volume.shape
     return conv.reshape(shape), gin.reshape(shape), jnp.transpose(gw, (1, 2, 0))
 

time: 50.4 us -> 44.4 us (0.88)
  local copies, waits for them, and re-layouts: 5.17 us -> 0 us
  Pallas kernels: 44.3 us -> 43.1 us
    unnamed x9 -> x0, local copies, waits for them, and re-layouts: 5.17 us -> none
    pallas_call x1, Pallas kernels: 44.3 us -> 42.4 us  [on_device(): pl.pallas_call(kernel, out_shape=(jax.ShapeDtypeStruct((BLOCK, CELLS), BF...]
    pallas_call x0 -> x1, Pallas kernels: none -> 0.72 us  [on_device(): pl.pallas_call(store, out_shape=tuple((jax.ShapeDtypeStruct(a.shape, a.dt...]
where the time goes in v3:
time: 44.4 us; the launch traced here: 43.8 us
  Pallas kernels  43.1 us (97%)
  between operations  0.64 us (1%)
    pallas_call x1, Pallas kernels, on_device(): pl.pallas_call(kernel, out_shape=(jax.ShapeDtypeStruct((BLOCK, CELLS), BF...  42.4 us

profile of v3, /device:TPU:1, one launch (start us, length us, event | category | flops | bytes accessed | tf_op | source)
XLA Modules:
  0.0 43.8 jit_solution(15149415453419677105)
XLA Ops:
  0.6 42.4 %shard_map.58 = (bf16[12,1024]{1,0:T(8,128)(2,1)S(1)}, bf16[12,1024]{1,0:T(8,128)(2,1)S(1)}, bf16[12,27,192]{2,1,0:T(8,128)(2,1)S(1)}) custom-call(bf16[12,1024]{1,0:T(8,128)(2,1)} %bitcast.5, bf16[27,192,192]{2,1,0:T(8,128)(2,1)} %w_ref.1, bf16[12,1024]{1,0:T(8,128)(2,1)} %bitcast.6), custom_call_target="tpu_custom_call" | custom-call | flops 400000000 | bytes 3000000 | tf_op jit(solution)/shard_map/pallas_call | solution.py:343
  43.1 0.7 %shard_map.59 = (bf16[12,1024]{1,0:T(8,128)(2,1)}, bf16[12,1024]{1,0:T(8,128)(2,1)}, bf16[12,27,192]{2,1,0:T(8,128)(2,1)}) custom-call(bf16[12,1024]{1,0:T(8,128)(2,1)S(1)} %get-tuple-element.9.conv_ref, bf16[12,1024]{1,0:T(8,128)(2,1)S(1)} %get-tuple-element.10.gin_ref, bf16[12,27,192]{2,1,0:T(8,128)(2,1)S(1)} %get-tuple-element.11.gw_ref), custom_call_target="tpu_custom_call" | custom-call | tf_op jit(solution)/shard_map/pallas_call | solution.py:381

commit v4 on v3

--- a/solution.py
+++ b/solution.py
@@ -27,6 +27,11 @@
 FIRST = ((0, 1), (1, 0), (1, 1))
 SECOND = ((3, 0), (3, 1), (2, 0), (2, 1))
 
+FAR_FIRST = sorted(
+    ((dy, dz) for dz in (2, 1, 3, 0) for dy in (4, 3, 5, 2, 6, 1, 7, 0) if dy or dz),
+    key=lambda at: -(min(at[0], 8 - at[0]) + 2 * min(at[1], 4 - at[1])),
+)
+
 
 def onehot(cond):
     return jnp.where(cond, 1.0, 0.0).astype(BF16)
@@ -91,12 +96,12 @@
     space = lax.axis_index("space")
     chan = lax.axis_index("chan")
     rep = lax.axis_index("rep")
-    core = lax.rem(chan, 2)
-    z_lo = lax.rem(chan // 2, 2)
-    x_at = chan // 4
+    core = chan & 1
+    z_lo = (chan >> 1) & 1
+    x_at = chan >> 2
     sibling = chan + 1 - 2 * core
-    up = lax.rem(space + 1, SPACE)
-    down = lax.rem(space + SPACE - 1, SPACE)
+    up = (space + 1) & 7
+    down = (space + 7) & 7
     me = space * REP + rep
 
     vol_copy = pltpu.make_async_copy(vol_ref, vol_in, in_sem.at[0])
@@ -107,18 +112,19 @@
     w_copy.start()
 
     def chip_at(dx, dz):
-        return lax.rem(x_at + dx, 4) * 4 + lax.rem(z_lo + dz, 2) * 2 + core
+        return ((x_at + dx) & 3) * 4 + ((z_lo + dz) & 1) * 2 + core
 
     barrier = pltpu.get_barrier_semaphore()
     for dx, dz in FIRST + SECOND:
         pl.semaphore_signal(barrier, inc=1, device_id={"chan": chip_at(dx, dz)}, device_id_type=MESH)
     pl.semaphore_signal(barrier, inc=1, device_id={"chan": sibling}, device_id_type=MESH)
-    for rel in range(1, MEMBERS):
+    for dz in range(2):
         pl.semaphore_signal(
-            barrier, inc=1,
-            device_id={
-                "space": lax.rem(space + rel // REP, SPACE), "rep": lax.rem(rep + rel % REP, REP)
-            },
+            barrier, inc=1, device_id={"chan": chip_at(2, dz) ^ 1}, device_id_type=MESH
+        )
+    for dy, dz in FAR_FIRST:
+        pl.semaphore_signal(
+            barrier, inc=1, device_id={"space": (space + dy) & 7, "rep": (rep + dz) & 3},
             device_id_type=MESH,
         )
 
@@ -128,7 +134,7 @@
     grad_copy.wait()
     own_grad = jnp.concatenate([grad_in[...].astype(F32), pad], axis=0)
     grads[0] = own_grad.astype(BF16)
-    pl.semaphore_wait(barrier, 7 + 1 + MEMBERS - 1)
+    pl.semaphore_wait(barrier, 7 + 1 + 2 + MEMBERS - 1)
 
     def send(src, dst, s_sem, r_sem, where):
         return pltpu.make_async_remote_copy(
@@ -146,17 +152,23 @@
         return send(buf.at[slot], buf.at[slot + 1], s_sem.at[slot // 2], r_sem.at[slot // 2],
                     {"chan": sibling})
 
+    def to_far_core(buf, dx, dz, s_sem, r_sem):
+        slot = dx * 4 + dz * 2
+        return send(buf.at[0], buf.at[slot + 1], s_sem.at[slot // 2], r_sem.at[slot // 2],
+                    {"chan": chip_at(4 - dx, dz) ^ 1})
+
     started = []
 
     def go(copy):
         copy.start()
         started.append(copy)
 
-    def pass_on(buf, group, sems):
+    def pass_on(buf, group, sems, direct=False):
         s_sem, r_sem, fs_sem, fr_sem = sems
         for dx, dz in group:
             to_peer(buf, dx, dz, s_sem, r_sem).wait_recv()
-            go(to_sibling(buf, dx, dz, fs_sem, fr_sem))
+            if not (direct and dx == 2):
+                go(to_sibling(buf, dx, dz, fs_sem, fr_sem))
         for dx, dz in group:
             to_sibling(buf, dx, dz, fs_sem, fr_sem).wait_recv()
 
@@ -171,6 +183,8 @@
     go(halo_down)
     for dx, dz in SECOND:
         go(to_peer(vols, dx, dz, vs, vr))
+        if dx == 2:
+            go(to_far_core(vols, dx, dz, fvs, fvr))
     for dx, dz in FIRST + SECOND:
         go(to_peer(grads, dx, dz, gs, gr))
     go(to_sibling(grads, 0, 0, fgs, fgr))
@@ -207,10 +221,10 @@
         parts[16 * half : 16 * half + 16] = jnp.concatenate([sums[:256], side], axis=1).reshape(
             16, 16, 128
         )
-        for k in range(4):
-            pair = lax.rem(space // 2 + k, 4)
-            for dz in range(REP):
-                y, z = 2 * pair + half, lax.rem(rep + dz, REP)
+        for dz in (2, 1, 3, 0):
+            for k in (2, 1, 3, 0):
+                pair = ((space >> 1) + k) & 3
+                y, z = 2 * pair + half, (rep + dz) & 3
                 copy = send(parts.at[16 * half + pair * REP + z], got.at[me], rs, rr,
                             {"space": y, "rep": z})
                 if k == 0 and dz == 0:
@@ -232,25 +246,25 @@
     w_copy.wait()
     picked = [dot_nt(mine, w_vmem[tap]).astype(BF16) for tap in range(TAPS)]
     w_out[...] = dot(jnp.concatenate(picked, axis=0), slot_of).astype(BF16)
-    pass_on(vols, SECOND, v_sems)
+    pass_on(vols, SECOND, v_sems, direct=True)
     scatter(1)
     picked = [dot(mine, w_vmem[tap]).astype(BF16) for tap in range(TAPS)]
     w_in[...] = dot(jnp.concatenate(picked, axis=0), slot_of).astype(BF16)
 
-    piece = lax.rem(space, 2) * 16 + (space // 2) * REP + rep
+    own_four = (space & 1) * 16 + (space >> 1) * REP
+    piece = own_four + rep
     bulk = pl.ds(0, MEMBERS - 1)
 
     def reduce_piece():
         got[me] = parts[piece]
         send(got.at[bulk], got.at[bulk], rs, rr, {"space": up}).wait_recv()
         final[piece] = (jnp.sum(got[...], axis=0) * FACTOR).astype(BF16)
-        for rel in range(1, MEMBERS):
+        for dy, dz in FAR_FIRST:
             send(final.at[piece], final.at[piece], as_, ar, {
-                "space": lax.rem(space + rel // REP, SPACE), "rep": lax.rem(rep + rel % REP, REP)
+                "space": (space + dy) & 7, "rep": (rep + dz) & 3
             }).start()
 
-    even = lax.rem(space, 2) == 0
-    pl.when(even)(reduce_piece)
+    even = (space & 1) == 0
 
 
     def exchange(slot, buf, side_at, where):
@@ -269,7 +283,7 @@
     exchange(2, in_sums, 0, up)
     in_sums[1] = depth_sums(w_in, grad_fields, -1, -1)
     exchange(3, in_sums, 1, down)
-    pl.when(jnp.logical_not(even))(reduce_piece)
+    reduce_piece()
     out_sums[4] = depth_sums(w_out, fields, 1, 0)
     in_sums[4] = depth_sums(w_in, grad_fields, -1, 0)
 

time: 44.4 us -> 43.1 us (0.971)
  Pallas kernels: 43.1 us -> 41.7 us
    pallas_call x1, Pallas kernels: 42.4 us -> 41 us  [on_device(): pl.pallas_call(kernel, out_shape=(jax.ShapeDtypeStruct((BLOCK, CELLS), BF...]
where the time goes in v4:
time: 43.1 us; the launch traced here: 42.3 us
  Pallas kernels  41.7 us (97%)
  between operations  0.64 us (1%)
    pallas_call x1, Pallas kernels, on_device(): pl.pallas_call(kernel, out_shape=(jax.ShapeDtypeStruct((BLOCK, CELLS), BF...  41 us

profile of v4, /device:TPU:1, one launch (start us, length us, event | category | flops | bytes accessed | tf_op | source)
XLA Modules:
  0.0 42.3 jit_solution(10882248436224070663)
XLA Ops:
  0.6 41.0 %shard_map.58 = (bf16[12,1024]{1,0:T(8,128)(2,1)S(1)}, bf16[12,1024]{1,0:T(8,128)(2,1)S(1)}, bf16[12,27,192]{2,1,0:T(8,128)(2,1)S(1)}) custom-call(bf16[12,1024]{1,0:T(8,128)(2,1)} %bitcast.5, bf16[27,192,192]{2,1,0:T(8,128)(2,1)} %w_ref.1, bf16[12,1024]{1,0:T(8,128)(2,1)} %bitcast.6), custom_call_target="tpu_custom_call" | custom-call | flops 400000000 | bytes 3000000 | tf_op jit(solution)/shard_map/pallas_call | solution.py:357
  41.6 0.7 %shard_map.59 = (bf16[12,1024]{1,0:T(8,128)(2,1)}, bf16[12,1024]{1,0:T(8,128)(2,1)}, bf16[12,27,192]{2,1,0:T(8,128)(2,1)}) custom-call(bf16[12,1024]{1,0:T(8,128)(2,1)S(1)} %get-tuple-element.9.conv_ref, bf16[12,1024]{1,0:T(8,128)(2,1)S(1)} %get-tuple-element.10.gin_ref, bf16[12,27,192]{2,1,0:T(8,128)(2,1)S(1)} %get-tuple-element.11.gw_ref), custom_call_target="tpu_custom_call" | custom-call | tf_op jit(solution)/shard_map/pallas_call | solution.py:395

commit v5 on v4

--- a/solution.py
+++ b/solution.py
@@ -276,14 +276,21 @@
     out_sums[1] = depth_sums(w_out, fields, 1, -1)
     exchange(1, out_sums, 1, up)
 
+    for dx, dz in FIRST:
+        to_peer(grads, dx, dz, gs, gr).wait_recv()
+        go(to_sibling(grads, dx, dz, fgs, fgr))
+    for dx, dz in SECOND:
+        to_peer(grads, dx, dz, gs, gr).wait_recv()
+        go(to_sibling(grads, dx, dz, fgs, fgr))
+    reduce_piece()
     to_sibling(grads, 0, 0, fgs, fgr).wait_recv()
-    pass_on(grads, FIRST + SECOND, g_sems)
+    for dx, dz in FIRST + SECOND:
+        to_sibling(grads, dx, dz, fgs, fgr).wait_recv()
     grad_fields = grads[...].reshape(CHAN * SLOT, CELLS)
     in_sums[0] = depth_sums(w_in, grad_fields, -1, 1)
     exchange(2, in_sums, 0, up)
     in_sums[1] = depth_sums(w_in, grad_fields, -1, -1)
     exchange(3, in_sums, 1, down)
-    reduce_piece()
     out_sums[4] = depth_sums(w_out, fields, 1, 0)
     in_sums[4] = depth_sums(w_in, grad_fields, -1, 0)
 

time: 43.1 us -> 43 us (level)
  no operation moved by 1% of the time
where the time goes in v5:
time: 43 us; the launch traced here: 42.3 us
  Pallas kernels  41.6 us (97%)
  between operations  0.64 us (1%)
    pallas_call x1, Pallas kernels, on_device(): pl.pallas_call(kernel, out_shape=(jax.ShapeDtypeStruct((BLOCK, CELLS), BF...  40.9 us

profile of v5, /device:TPU:1, one launch (start us, length us, event | category | flops | bytes accessed | tf_op | source)
XLA Modules:
  0.0 42.3 jit_solution(340653898051587400)
XLA Ops:
  0.6 40.9 %shard_map.58 = (bf16[12,1024]{1,0:T(8,128)(2,1)S(1)}, bf16[12,1024]{1,0:T(8,128)(2,1)S(1)}, bf16[12,27,192]{2,1,0:T(8,128)(2,1)S(1)}) custom-call(bf16[12,1024]{1,0:T(8,128)(2,1)} %bitcast.5, bf16[27,192,192]{2,1,0:T(8,128)(2,1)} %w_ref.1, bf16[12,1024]{1,0:T(8,128)(2,1)} %bitcast.6), custom_call_target="tpu_custom_call" | custom-call | flops 400000000 | bytes 3000000 | tf_op jit(solution)/shard_map/pallas_call | solution.py:364
  41.6 0.7 %shard_map.59 = (bf16[12,1024]{1,0:T(8,128)(2,1)}, bf16[12,1024]{1,0:T(8,128)(2,1)}, bf16[12,27,192]{2,1,0:T(8,128)(2,1)}) custom-call(bf16[12,1024]{1,0:T(8,128)(2,1)S(1)} %get-tuple-element.9.conv_ref, bf16[12,1024]{1,0:T(8,128)(2,1)S(1)} %get-tuple-element.10.gin_ref, bf16[12,27,192]{2,1,0:T(8,128)(2,1)S(1)} %get-tuple-element.11.gw_ref), custom_call_target="tpu_custom_call" | custom-call | tf_op jit(solution)/shard_map/pallas_call | solution.py:402
